TPU v7x, 512 devices: a whole 4x4x16 slice. The times are simulated.
512 devices in a mesh: patch: 64 (over z, x_lo, core), img: 8 (over y, x_hi).
Axes of the slice: x: 4 (x_hi: 2, x_lo: 2; x = x_hi * 2 + x_lo), y: 4, z: 16, core: 2. Of those that a mesh axis runs over, the one named last changes fastest.
Arguments:
- latents: bfloat16 [65536, 640], P(('img', 'patch')), parts along dimension 0, may hold values from -16 to 16
- stale_keys: bfloat16 [65536, 320], P(('img', 'patch')), parts along dimension 0, may hold values from -6 to 6
- stale_values: bfloat16 [65536, 320], P(('img', 'patch')), parts along dimension 0, may hold values from -6 to 6
- timestep: int32 [1], replicated, may hold values from 0 to 999
- text_ids: int32 [616], P('img'), parts along dimension 0, may hold values from 0 to 24703
- text_table: bfloat16 [24704, 1280], P('patch'), may hold values from -24 to 24
- time_weight: bfloat16 [1280, 640], replicated, may hold values from -0.15625 to 0.15625
- norm_gain: float32 [640], replicated, may hold values from 0.5 to 1.5
- norm_bias: float32 [640], replicated, may hold values from -3 to 3
- w_query: bfloat16 [640, 320], replicated, may hold values from -0.25 to 0.25
- w_key: bfloat16 [640, 320], replicated, may hold values from -0.25 to 0.25
- w_value: bfloat16 [640, 320], replicated, may hold values from -0.25 to 0.25
- w_out: bfloat16 [320, 640], replicated, may hold values from -1.25 to 1.25
Outputs:
- mixed: bfloat16 [65536, 640], P(('img', 'patch')), parts along dimension 0
- fresh_keys: bfloat16 [65536, 320], P(('img', 'patch')), parts along dimension 0
- fresh_values: bfloat16 [65536, 320], P(('img', 'patch')), parts along dimension 0
There are 8 independent parts, one for each index of `img`. A program takes and returns all parts, laid end to end along the dimension named above; an argument that names none is the same for every part. Nothing has to cross between parts.
All inputs are finite; a program needn't handle non-finite values.
Results may differ from a plain program's by a relative error of at most 0.0051.
Values may be sent and summed in bfloat16 or wider, within the bound.
A program may use at most 128 MiB of HBM per device.

v0:
```python
import math

import jax
import jax.numpy as jnp
from jax import lax
from jax.sharding import PartitionSpec as P

HEAD_DIM = 64
GROUPS = 32


def embed_time(timestep, width):
    half = width // 2
    freq = jnp.exp(-math.log(10000.0) * jnp.arange(half, dtype=jnp.float32) / half)
    angle = timestep[0].astype(jnp.float32) * freq
    return jnp.concatenate([jnp.cos(angle), jnp.sin(angle)])


def head_scores(query_f, keys, heads):
    key_f = keys.astype(jnp.float32).reshape(keys.shape[0], heads, HEAD_DIM)
    return jnp.einsum("qhd,khd->hqk", query_f, key_f) * (1.0 / math.sqrt(HEAD_DIM))


def head_values(probs, values, heads):
    value_f = values.astype(jnp.float32).reshape(values.shape[0], heads, HEAD_DIM)
    return jnp.einsum("hqk,khd->hqd", probs, value_f)


def on_device(
    latents,
    stale_keys,
    stale_values,
    timestep,
    text_ids,
    text_table,
    time_weight,
    norm_gain,
    norm_bias,
    w_query,
    w_key,
    w_value,
    w_out,
):
    parts = lax.axis_size("patch")
    mine = lax.axis_index("patch")
    tok, width = latents.shape
    att = w_query.shape[1]
    heads = att // HEAD_DIM
    voc_rows = text_table.shape[0]
    local_ids = text_ids - mine * voc_rows
    onehot = (local_ids[:, None] == jnp.arange(voc_rows, dtype=jnp.int32)[None, :]).astype(
        jnp.bfloat16
    )
    partial_pool = jnp.sum(jnp.dot(onehot, text_table, preferred_element_type=jnp.float32), axis=0)
    pooled = lax.psum(partial_pool, "patch") / text_ids.shape[0]
    temb = embed_time(timestep, time_weight.shape[0])
    cond = jax.nn.silu(temb + pooled).astype(jnp.bfloat16)
    shift = jnp.dot(cond[None, :], time_weight, preferred_element_type=jnp.float32)[0]
    shifted = latents.astype(jnp.float32) + shift[None, :]
    grouped = shifted.reshape(tok, GROUPS, width // GROUPS)
    count = tok * parts * (width // GROUPS)
    total = lax.psum(jnp.sum(grouped, axis=(0, 2)), "patch")
    mean = total / count
    centered = grouped - mean[None, :, None]
    var = lax.psum(jnp.sum(centered * centered, axis=(0, 2)), "patch") / count
    normed = (centered * lax.rsqrt(var + 1e-05)[None, :, None]).reshape(
        tok, width
    ) * norm_gain + norm_bias
    normed = normed.astype(jnp.bfloat16)
    queries = jnp.dot(normed, w_query, preferred_element_type=jnp.float32).astype(jnp.bfloat16)
    fresh_keys = jnp.dot(normed, w_key, preferred_element_type=jnp.float32).astype(jnp.bfloat16)
    fresh_values = jnp.dot(normed, w_value, preferred_element_type=jnp.float32).astype(jnp.bfloat16)
    query_f = queries.astype(jnp.float32).reshape(tok, heads, HEAD_DIM)
    own = head_scores(query_f, fresh_keys, heads)
    top = jnp.max(own, axis=-1)
    probs = jnp.exp(own - top[..., None])
    mass = jnp.sum(probs, axis=-1)
    accum = head_values(probs, fresh_values, heads)
    low = mine * tok
    piece_keys = lax.all_gather(stale_keys, "patch", axis=0, tiled=True)
    piece_values = lax.all_gather(stale_values, "patch", axis=0, tiled=True)
    count_rows = piece_keys.shape[0]
    position = jnp.arange(count_rows, dtype=jnp.int32)
    inside = (position >= low) & (position < low + tok)
    scores = head_scores(query_f, piece_keys, heads)
    scores = jnp.where(inside[None, None, :], -jnp.inf, scores)
    new_max = jnp.maximum(top, jnp.max(scores, axis=-1))
    factor = jnp.exp(top - new_max)
    weights = jnp.exp(scores - new_max[..., None])
    new_mass = mass * factor + jnp.sum(weights, axis=-1)
    new_acc = accum * factor[..., None] + head_values(weights, piece_values, heads)
    result = new_acc / new_mass[..., None]
    attended = jnp.transpose(result, (1, 0, 2)).reshape(tok, att).astype(jnp.bfloat16)
    mixed = shifted + jnp.dot(attended, w_out, preferred_element_type=jnp.float32)
    return (mixed.astype(jnp.bfloat16), fresh_keys, fresh_values)


def solution(mesh):
    return jax.shard_map(
        on_device,
        mesh=mesh,
        in_specs=(
            P(("img", "patch"), None),
            P(("img", "patch"), None),
            P(("img", "patch"), None),
            P(),
            P("img"),
            P("patch", None),
            P(),
            P(),
            P(),
            P(),
            P(),
            P(),
            P(),
        ),
        out_specs=(P(("img", "patch"), None), P(("img", "patch"), None), P(("img", "patch"), None)),
        check_vma=False,
    )
```

profile of v0, /device:TPU:1, one launch (start us, length us, event | category | flops | bytes accessed | tf_op | source)
XLA Modules:
  0.0 384.3 jit_solution(2571419396812839669)
XLA Ops:
  7.2 0.7 all-gather.3.cloned.1.call-update
  8.0 0.7 all-gather.5.cloned.1.call-update
  9.3 0.7 broadcast_subtract_fusion
  10.0 1.7 convolution_reduce_fusion
  11.6 115.2 %psum.21 = f32[1280]{0:T(1024)S(1)} all-reduce(f32[1280]{0:T(1024)S(1)} %convolution_reduce_fusion), channel_id=1, replica_groups=mesh['patch'=64,'img'=8] {'patch'}, use_global_device_ids=true, to_apply=%region_1.0 | all-reduce | flops 1280 | bytes 10240 | tf_op jit(solution)/shard_map/psum | solution.py:55
  127.0 0.3 convolution_reduce_fusion.1
  127.3 1.0 fusion.14
  128.4 0.1 reduce_sum.66
  128.5 108.0 %psum.22 = f32[32]{0:T(128)S(1)} all-reduce(f32[32]{0:T(128)S(1)} %reduce_sum.66), channel_id=1, replica_groups=mesh['patch'=64,'img'=8] {'patch'}, use_global_device_ids=true, to_apply=%region_4.5 | all-reduce | flops 32 | bytes 256 | tf_op jit(solution)/shard_map/psum | solution.py:62
  236.6 0.1 sub.51
  236.7 1.0 multiply_reduce_fusion
  237.7 0.1 reduce_sum.69
  237.9 104.9 %psum.23 = f32[32]{0:T(128)S(1)} all-reduce(f32[32]{0:T(128)S(1)} %reduce_sum.69), channel_id=1, replica_groups=mesh['patch'=64,'img'=8] {'patch'}, use_global_device_ids=true, to_apply=%region_7.8 | all-reduce | flops 32 | bytes 256 | tf_op jit(solution)/shard_map/psum | solution.py:65
  342.8 0.1 mul.78
  343.0 1.4 convolution_convert_fusion.1
  344.4 1.4 convolution_convert_fusion.2
  345.9 0.3 fusion.25
  346.2 1.4 convolution_convert_fusion
  347.7 5.1 %fusion = (f32[5,128]{1,0:T(8,128)S(1)}, f32[5,128,8192]{2,1,0:T(8,128)S(1)}) fusion(pred[8192]{0:T(1024)(128)(4,1)S(1)} %fusion.18, bf16[128,5,64]{0,2,1:T(8,128)(2,1)S(1)} %bitcast.47, bf16[8192,5,64]{0,2,1:T(8,128)(2,1)} %bitcast.45), kind=kOutput, calls=%fused_computation.2 | convolution fusion | flops 686816640 | bytes 26307072 | tf_op jit(solution)/shard_map/qhd,khd->hqk/dot_general | solution.py:21
  352.8 7.0 %copy-done.1 = f32[5,128,8192]{2,1,0:T(8,128)} copy-done((f32[5,128,8192]{2,1,0:T(8,128)}, f32[5,128,8192]{2,1,0:T(8,128)S(1)}, u32[]{:S(2)}) %copy-start.1) | copy-done | bytes 20971544
  359.8 5.5 %fusion.1 = f32[5,128]{1,0:T(8,128)S(1)} fusion(f32[5,128,8192]{2,1,0:T(8,128)S(1)} %get-tuple-element.8, f32[5,128]{1,0:T(8,128)S(1)} %max.18, pred[8192]{0:T(1024)(128)(4,1)S(1)} %fusion.18), kind=kLoop, calls=%fused_computation.3 | loop fusion | flops 20970880 | bytes 20984832 | tf_op jit(solution)/shard_map/reduce_sum | solution.py:90
  365.4 10.9 %fusion.11 = f32[128,5,64]{0,2,1:T(8,128)S(1)} fusion(bf16[8192,5,64]{0,2,1:T(8,128)(2,1)} %bitcast.50, f32[5,128,8192]{2,1,0:T(8,128)} %copy-done.1, f32[5,128]{1,0:T(8,128)S(1)} %max.18, pred[8192]{0:T(1024)(128)(4,1)S(1)} %fusion.18), kind=kOutput, calls=%fused_computation.17 | convolution fusion | flops 686817280 | bytes 26388992 | tf_op jit(solution)/shard_map/hqk,khd->hqd/dot_general | solution.py:26
  376.3 0.2 fusion.12
  376.5 1.0 fusion.7
  (28 shorter events, 0.7 us)
Async XLA Ops:
  7.2 119.8 %copy-start = (bf16[1280,640]{1,0:T(8,128)(2,1)S(1)}, bf16[1280,640]{1,0:T(8,128)(2,1)}, u32[]{:S(2)}) copy-start(bf16[1280,640]{1,0:T(8,128)(2,1)} %param.19) | copy-start | bytes 4915204
  7.2 340.5 %all-gather.3.cloned.1.call-start = ((), (), s32[]{:S(2)}) async-start(), calls=%async_computation | async-start | bytes 5324800 | tf_op jit(solution)/shard_map/all_gather | solution.py:80
  7.9 357.4 %all-gather.5.cloned.1.call-start = ((), (), s32[]{:S(2)}) async-start(), calls=%async_computation.1 | async-start | bytes 5324800 | tf_op jit(solution)/shard_map/all_gather | solution.py:81
  344.4 20.9 %copy-start.4 = (bf16[128,320]{0,1:T(8,128)(2,1)}, bf16[128,320]{0,1:T(8,128)(2,1)S(1)}, u32[]{:S(2)}) copy-start(bf16[128,320]{0,1:T(8,128)(2,1)S(1)} %convolution_convert_fusion.1) | copy-start | bytes 245764
  347.6 28.6 %copy-start.5 = (bf16[128,320]{0,1:T(8,128)(2,1)}, bf16[128,320]{0,1:T(8,128)(2,1)S(1)}, u32[]{:S(2)}) copy-start(bf16[128,320]{0,1:T(8,128)(2,1)S(1)} %convolution_convert_fusion) | copy-start | bytes 245764
  352.8 7.0 %copy-start.1 = (f32[5,128,8192]{2,1,0:T(8,128)}, f32[5,128,8192]{2,1,0:T(8,128)S(1)}, u32[]{:S(2)}) copy-start(f32[5,128,8192]{2,1,0:T(8,128)S(1)} %get-tuple-element.8) | copy-start | bytes 62914564
  365.4 11.1 %copy-start.2 = (bf16[128,640]{1,0:T(8,128)(2,1)S(1)}, bf16[128,640]{1,0:T(8,128)(2,1)}, u32[]{:S(2)}) copy-start(bf16[128,640]{1,0:T(8,128)(2,1)} %param.13) | copy-start | bytes 491524
  365.4 11.1 %copy-start.3 = (bf16[320,640]{1,0:T(8,128)(2,1)S(1)}, bf16[320,640]{1,0:T(8,128)(2,1)}, u32[]{:S(2)}) copy-start(bf16[320,640]{1,0:T(8,128)(2,1)} %param.25) | copy-start | bytes 1228804
Sparse Core Ops, SparseCore 0:
  10.1 137.9 all-gather.2
  150.1 127.0 all-gather.4
where the time goes:
time: 385 us; the launch traced here: 384 us
  blocking collectives  328 us (85%)
  matrix products  23.7 us (6%)
  between operations  14.9 us (4%)
  other arithmetic  8.56 us (2%)
  local copies, waits for them, and re-layouts  7.54 us (2%)
    psum x1, blocking collectives, on_device(): pooled = lax.psum(partial_pool, 'patch') / text_ids.shape[0]  115 us
    psum x1, blocking collectives, on_device(): total = lax.psum(jnp.sum(grouped, axis=(0, 2)), 'patch')  108 us
    psum x1, blocking collectives, on_device(): var = lax.psum(jnp.sum(centered * centered, axis=(0, 2)), 'patch') / count  105 us
    dot_general x2, matrix products, head_values(): return jnp.einsum('hqk,khd->hqd', probs, value_f)  11.1 us
  transfers between devices with their start and end apart: 2, of which 0 were waited for; matrix products, arithmetic and copies ran while one was open for 5% of the time, Pallas kernels for 0%

commit v1 on v0

v1 whole, which is shorter than its diff:
```python
import functools
import math

import jax
import jax.numpy as jnp
from jax import lax
from jax.experimental import pallas as pl
from jax.experimental.pallas import tpu as pltpu
from jax.sharding import PartitionSpec as P

HEAD_DIM = 64
GROUPS = 32
QUAD = 4
LANE = 128
MESH = pl.DeviceIdType.MESH
BF16 = jnp.bfloat16
F32 = jnp.float32


def dot(a, b):
    return jnp.dot(a, b, preferred_element_type=F32)


def dot_nt(a, b):
    return lax.dot_general(a, b, (((1,), (1,)), ((), ())), preferred_element_type=F32)


def iota(shape, axis):
    return lax.broadcasted_iota(jnp.int32, shape, axis)


def eye(rows, cols, shift=0):
    return (iota((rows, cols), 0) + shift == iota((rows, cols), 1)).astype(BF16)


def pieces(x):
    high = x.astype(BF16).astype(F32)
    rest = x - high
    mid = rest.astype(BF16).astype(F32)
    return high, mid, rest - mid


def kernel(
    nz,
    text,
    time_ref,
    ids_ref,
    table_ref,
    gain_ref,
    bias_ref,
    lat_hbm,
    sk_hbm,
    sv_hbm,
    tw_hbm,
    wq_hbm,
    wk_hbm,
    wv_hbm,
    wo_hbm,
    mixed_hbm,
    fk_hbm,
    fv_hbm,
    lat,
    sk,
    tw,
    wq,
    wk,
    wv,
    wo,
    kv,
    stat,
    st1,
    st2,
    st3,
    qx,
    qp,
    acc,
    top,
    partial,
    arrived,
    fk,
    fv,
    mixed,
    group,
    in_sem,
    out_sem,
    up_send,
    up_recv,
    dn_send,
    dn_recv,
    s1_send,
    s1_recv,
    s2_send,
    s2_recv,
    s3_send,
    s3_recv,
    q_send,
    q_recv,
    o_send,
    o_recv,
):
    tok, width = lat.shape
    att = sk.shape[0]
    heads = att // HEAD_DIM
    me = lax.axis_index("patch")
    z = lax.div(me, QUAD)
    c = lax.rem(me, QUAD)

    def at(zz, cc):
        return {"patch": zz * QUAD + cc}

    def quad_to(j):
        return at(z, lax.rem(c + j, QUAD))

    def quad_from(j):
        return at(z, lax.rem(c + QUAD - j, QUAD))

    def along(j):
        return at(lax.rem(z + j, nz), c)

    def remote(src, dst, send, recv, who):
        return pltpu.make_async_remote_copy(
            src_ref=src, dst_ref=dst, send_sem=send, recv_sem=recv, device_id=who, device_id_type=MESH
        )

    loads = [
        pltpu.make_async_copy(src, dst, in_sem.at[i])
        for i, (src, dst) in enumerate(
            [
                (sk_hbm, sk),
                (sv_hbm, kv.at[0, pl.ds(att, att)]),
                (lat_hbm, lat),
                (tw_hbm, tw),
                (wq_hbm, wq),
                (wk_hbm, wk),
                (wv_hbm, wv),
                (wo_hbm, wo),
            ]
        )
    ]
    for load in loads:
        load.start()

    barrier = pltpu.get_barrier_semaphore()
    for j in range(1, QUAD):
        pl.semaphore_signal(barrier, inc=1, device_id=quad_to(j), device_id_type=MESH)
    for j in range(1, nz):
        pl.semaphore_signal(barrier, inc=1, device_id=along(j), device_id_type=MESH)

    def fill_keys(slot, keys):
        kv[slot, 0:128] = keys[:, 0:128]
        kv[slot, 128:256] = keys[:, 128:256]
        early, late = keys[0:64, 256:320], keys[64:128, 256:320]
        tail = dot(early, eye(64, LANE)) + dot(late, eye(64, LANE, 64))
        kv[slot, 256:320] = tail.astype(BF16)

    loads[0].wait()
    fill_keys(0, dot_nt(eye(tok, tok), sk[...]).astype(BF16))
    loads[1].wait()
    pl.semaphore_wait(barrier, QUAD - 1 + nz - 1)

    chunks = nz - 1
    reach = nz // 2

    def slot_up(d):
        return 0 if d == 0 else 2 * d - 1

    def slot_dn(d):
        return 0 if d == 0 else (2 * d if d < reach else 2 * d - 1)

    def ring(k, up):
        d = k // 2 + 1
        part = k % 2
        if k == chunks - 1:
            part = 0 if up else 1
        rows = pl.ds(part * att, att)
        place = slot_up if up else slot_dn
        send, recv = (up_send, up_recv) if up else (dn_send, dn_recv)
        return remote(
            kv.at[place(d - 1), rows],
            kv.at[place(d), rows],
            send.at[k],
            recv.at[k],
            along(1 if up else nz - 1),
        )

    done = [0]

    def service(count):
        for _ in range(count):
            k = done[0]
            if k >= chunks:
                return
            for up in (True, False):
                ring(k, up).wait_recv()
                if k + 2 < chunks - 1:
                    ring(k + 2, up).start()
                elif k == chunks - 3 and up or k == chunks - 2 and not up:
                    ring(chunks - 1, up).start()
            done[0] = k + 1

    def ensure(count):
        service(min(count, chunks) - done[0])

    for k in range(min(2, chunks)):
        for up in (True, False):
            ring(k, up).start()

    loads[2].wait()
    lat32 = lat[...].astype(F32)
    mean = jnp.sum(lat32, axis=0, keepdims=True) * (1.0 / tok)
    dev = lat32 - mean
    spread = jnp.sum(dev * dev, axis=0, keepdims=True)
    rows = table_ref.shape[0]
    hot = (iota((rows, text), 0) + me * rows == ids_ref[...]).astype(BF16)
    counts = dot_nt(jnp.ones((16, text), BF16), hot)
    pool = dot(counts.astype(BF16), table_ref[...])[0:1]
    temb_w = pool.shape[1]
    pq, mq = 384, 256
    pool = jnp.concatenate([pool, jnp.zeros((1, QUAD * pq - temb_w), F32)], axis=1)
    mean = jnp.concatenate([mean, jnp.zeros((1, QUAD * mq - width), F32)], axis=1)
    spread = jnp.concatenate([spread, jnp.zeros((1, QUAD * mq - width), F32)], axis=1)
    for q in range(QUAD):
        stat[q, :, 0:pq] = pool[:, q * pq : (q + 1) * pq]
        stat[q, :, pq : pq + mq] = mean[:, q * mq : (q + 1) * mq]
        stat[q, :, pq + mq : pq + 2 * mq] = spread[:, q * mq : (q + 1) * mq]

    first = [
        remote(stat.at[lax.rem(c + j, QUAD)], st1.at[j], s1_send.at[j], s1_recv.at[j], quad_to(j))
        for j in range(1, QUAD)
    ]
    for copy in first:
        copy.start()
    st1[0] = stat[c]

    per = width // GROUPS
    gr = jnp.floor((iota((width, width), 0).astype(F32) + 0.5) * (1.0 / per))
    gc = jnp.floor((iota((width, width), 1).astype(F32) + 0.5) * (1.0 / per))
    group[...] = (gr == gc).astype(BF16)
    half = temb_w // 2
    freq = jnp.exp(-math.log(10000.0) * iota((1, half), 1).astype(F32) / half)
    angle = time_ref[0].astype(F32) * freq
    temb = jnp.concatenate([jnp.cos(angle), jnp.sin(angle)], axis=1)

    def merge(ref, n):
        x = ref[...]
        count = x.shape[0]
        p = jnp.sum(x[:, :, 0:pq], axis=0)
        ms = x[:, :, pq : pq + mq]
        m = jnp.sum(ms, axis=0) * (1.0 / count)
        off = ms - m[None]
        v = jnp.sum(x[:, :, pq + mq : pq + 2 * mq], axis=0) + n * jnp.sum(off * off, axis=0)
        return p, m, v

    def put(ref, slot, three):
        p, m, v = three
        ref[slot, :, 0:pq] = p
        ref[slot, :, pq : pq + mq] = m
        ref[slot, :, pq + mq : pq + 2 * mq] = v

    for copy in first:
        copy.wait()
    put(st2, 0, merge(st1, float(tok)))
    second = [
        remote(st2.at[0], st2.at[j], s2_send.at[j], s2_recv.at[j], along(j)) for j in range(1, nz)
    ]
    for copy in second:
        copy.start()
    service(1)
    for copy in second:
        copy.wait()
    put(st3, c, merge(st2, float(tok * QUAD)))
    third = [
        remote(st3.at[c], st3.at[c], s3_send.at[j], s3_recv.at[j], quad_to(j))
        for j in range(1, QUAD)
    ]
    for copy in third:
        copy.start()
    service(2)
    for j in range(1, QUAD):
        third[j - 1].wait_send()
        owner = lax.rem(c + QUAD - j, QUAD)
        remote(st3.at[owner], st3.at[owner], s3_send.at[j], s3_recv.at[j], quad_from(j)).wait_recv()

    total = [st3[q] for q in range(QUAD)]
    pool = jnp.concatenate([t[:, 0:pq] for t in total], axis=1)[:, 0:temb_w]
    mean = jnp.concatenate([t[:, pq : pq + mq] for t in total], axis=1)[:, 0:width]
    spread = jnp.concatenate([t[:, pq + mq : pq + 2 * mq] for t in total], axis=1)[:, 0:width]

    cond = jax.nn.silu(temb + pool * (1.0 / text)).astype(BF16)
    loads[3].wait()
    shift = dot(jnp.broadcast_to(cond, (16, temb_w)), tw[...])[0:1]

    def group_mean(x):
        a, b, d = pieces(x)
        row = iota((16, width), 0)
        stacked = jnp.where(row == 0, a, jnp.where(row == 1, b, jnp.where(row == 2, d, 0.0)))
        return jnp.sum(dot(stacked.astype(BF16), group[...]), axis=0, keepdims=True) * (1.0 / per)

    service(1)
    centre = mean + shift
    centre_g = group_mean(centre)
    off = centre - centre_g
    var = group_mean(spread * (1.0 / (tok * QUAD * nz)) + off * off)
    scale = lax.rsqrt(var + 1e-5) * gain_ref[...].reshape(1, width)
    offset = (shift - centre_g) * scale + bias_ref[...].reshape(1, width)
    normed = (lat[...].astype(F32) * scale + offset).astype(BF16)
    service(1)

    loads[4].wait()
    qx[0] = dot_nt(wq[...], normed).astype(BF16)
    asks = [
        remote(qx.at[0], qx.at[j], q_send.at[j], q_recv.at[j], quad_to(j)) for j in range(1, QUAD)
    ]
    for copy in asks:
        copy.start()
    loads[5].wait()
    loads[6].wait()
    fk[...] = dot_nt(wk[...], normed).astype(BF16)
    fv[...] = dot_nt(wv[...], normed).astype(BF16)
    fresh_out = [
        pltpu.make_async_copy(fk, fk_hbm, out_sem.at[0]),
        pltpu.make_async_copy(fv, fv_hbm, out_sem.at[1]),
    ]
    for copy in fresh_out:
        copy.start()
    fill_keys(nz, dot_nt(eye(tok, tok), fk[...]).astype(BF16))
    kv[nz, pl.ds(att, att)] = fv[...]
    service(1)

    blank = jnp.zeros((64, tok), BF16)

    def place_queries(j):
        cols = pl.ds(j * tok, tok)
        for h in range(heads + 1):
            own = qx[j, min(h, 4) * 64 : min(h, 4) * 64 + 64]
            qp[h, 0:64, cols] = own if h % 2 == 0 else blank
            qp[h, 64:128, cols] = blank if h % 2 == 0 else own

    log2e = 0.125 * math.log2(math.e)

    def attend(h, q0, nq, parts, start):
        cols = pl.ds(q0, nq)
        count = sum(b - a for a, b in parts)

        def rows_of(r0, n):
            got = [kv[a:b, r0 : r0 + n].reshape((b - a) * n, LANE) for a, b in parts]
            return got[0] if len(got) == 1 else jnp.concatenate(got, axis=0)

        if h < 4:
            s = dot(rows_of((h // 2) * LANE, LANE), qp[h, :, cols])
        else:
            keys = rows_of(256, 64)
            early = dot(keys, qp[4, :, cols]).reshape(count, 64, nq)
            late = dot(keys, qp[5, :, cols]).reshape(count, 64, nq)
            s = jnp.concatenate([early, late], axis=1).reshape(count * tok, nq)
        m = jnp.max(s, axis=0, keepdims=True) * log2e
        if not start:
            old = top[h, 0:1, cols]
            m = jnp.maximum(old, m)
            fade = jnp.exp2(old - m)
        p = jnp.exp2(s * log2e - m).astype(BF16)
        r0 = att + h * 64
        values = [kv[i, r0 : r0 + 64] for a, b in parts for i in range(a, b)]
        values = values[0] if count == 1 else jnp.concatenate(values, axis=1)
        ones = jnp.ones((16, count * tok), BF16)
        out = dot(jnp.concatenate([values, ones], axis=0), p)[0:72]
        acc[h, :, cols] = out if start else acc[h, :, cols] * fade + out
        top[h, :, cols] = jnp.broadcast_to(m, (8, nq))

    reach_a = max(1, reach - 4)
    end_a = 2 * reach_a + 1
    ensure(2 * reach_a)
    place_queries(0)
    for h in range(heads):
        attend(h, 0, tok, [(nz, nz + 1), (1, end_a)], True)
    for copy in asks:
        copy.wait()
    for j in range(1, QUAD):
        place_queries(j)
    for h in range(heads):
        attend(h, tok, 3 * tok, [(0, end_a)], True)
        if h < 4:
            service(1)
    reach_b = reach - 2
    if reach_b > reach_a:
        end_b = 2 * reach_b + 1
        ensure(2 * reach_b)
        for h in range(heads):
            attend(h, 0, QUAD * tok, [(end_a, end_b)], False)
            if h % 2 == 1:
                service(1)
        end_a = end_b
    ensure(chunks)

    def finish(j, h):
        cols = pl.ds(j * tok, tok)
        weight = acc[h, 64:65, cols]
        return acc[h, 0:64, cols] / weight, top[h, 0:1, cols] + jnp.log2(weight)

    for h in range(heads):
        attend(h, tok, 3 * tok, [(end_a, nz)], False)
    replies = []
    row = iota((16, tok), 0)
    for j in range(1, QUAD):
        logs = jnp.zeros((16, tok), F32)
        for h in range(heads):
            o, log = finish(j, h)
            partial[j, h * 64 : h * 64 + 64] = o.astype(BF16)
            for i, x in enumerate(pieces(log)):
                logs = jnp.where(row == 3 * h + i, x, logs)
        partial[j, att : att + 16] = logs.astype(BF16)
        reply = remote(partial.at[j], arrived.at[j], o_send.at[j], o_recv.at[j], quad_from(j))
        reply.start()
        replies.append(reply)
    for h in range(heads):
        attend(h, 0, tok, [(end_a, nz)], False)
    own = [finish(0, h) for h in range(heads)]
    for reply in replies:
        reply.wait()
    attended = []
    peer_logs = [arrived[j, att : att + 16].astype(F32) for j in range(1, QUAD)]
    for h in range(heads):
        ls = [own[h][1]]
        for p in peer_logs:
            ls.append(p[3 * h : 3 * h + 1] + p[3 * h + 1 : 3 * h + 2] + p[3 * h + 2 : 3 * h + 3])
        os = [own[h][0]] + [arrived[j, h * 64 : h * 64 + 64].astype(F32) for j in range(1, QUAD)]
        big = jnp.maximum(jnp.maximum(ls[0], ls[1]), jnp.maximum(ls[2], ls[3]))
        ws = [jnp.exp2(x - big) for x in ls]
        num = ws[0] * os[0] + ws[1] * os[1] + ws[2] * os[2] + ws[3] * os[3]
        attended.append((num / (ws[0] + ws[1] + ws[2] + ws[3])).astype(BF16))
    attended = dot_nt(eye(tok, tok), jnp.concatenate(attended, axis=0)).astype(BF16)
    loads[7].wait()
    mixed[...] = (lat[...].astype(F32) + shift + dot(attended, wo[...])).astype(BF16)
    last = pltpu.make_async_copy(mixed, mixed_hbm, out_sem.at[2])
    last.start()
    for k in range(chunks):
        for up in (True, False):
            ring(k, up).wait_send()
    for copy in fresh_out:
        copy.wait()
    last.wait()


def solution(mesh):
    nz = mesh.shape["patch"] // QUAD

    def on_device(
        latents,
        stale_keys,
        stale_values,
        timestep,
        text_ids,
        text_table,
        time_weight,
        norm_gain,
        norm_bias,
        w_query,
        w_key,
        w_value,
        w_out,
    ):
        tok, width = latents.shape
        att = w_query.shape[1]
        temb_w = time_weight.shape[0]
        text = text_ids.shape[0]
        vmem = pl.BlockSpec(memory_space=pltpu.VMEM)
        smem = pl.BlockSpec(memory_space=pltpu.SMEM)
        hbm = pl.BlockSpec(memory_space=pl.ANY)
        chunks = nz - 1
        dma = pltpu.SemaphoreType.DMA
        scratch = [
            pltpu.VMEM((tok, width), BF16),
            pltpu.VMEM((att, tok), BF16),
            pltpu.VMEM((temb_w, width), BF16),
            pltpu.VMEM((att, width), BF16),
            pltpu.VMEM((att, width), BF16),
            pltpu.VMEM((att, width), BF16),
            pltpu.VMEM((att, width), BF16),
            pltpu.VMEM((nz + 1, 2 * att, tok), BF16),
            pltpu.VMEM((QUAD, 1, 896), F32),
            pltpu.VMEM((QUAD, 1, 896), F32),
            pltpu.VMEM((nz, 1, 896), F32),
            pltpu.VMEM((QUAD, 1, 896), F32),
            pltpu.VMEM((QUAD, att, tok), BF16),
            pltpu.VMEM((6, LANE, QUAD * tok), BF16),
            pltpu.VMEM((5, 72, QUAD * tok), F32),
            pltpu.VMEM((5, 8, QUAD * tok), F32),
            pltpu.VMEM((QUAD, att + 16, tok), BF16),
            pltpu.VMEM((QUAD, att + 16, tok), BF16),
            pltpu.VMEM((att, tok), BF16),
            pltpu.VMEM((att, tok), BF16),
            pltpu.VMEM((tok, width), BF16),
            pltpu.VMEM((width, width), BF16),
            dma((8,)),
            dma((3,)),
            dma((chunks,)),
            dma((chunks,)),
            dma((chunks,)),
            dma((chunks,)),
            dma((QUAD,)),
            dma((QUAD,)),
            dma((nz,)),
            dma((nz,)),
            dma((QUAD,)),
            dma((QUAD,)),
            dma((QUAD,)),
            dma((QUAD,)),
            dma((QUAD,)),
            dma((QUAD,)),
        ]
        mixed, fresh_keys, fresh_values = pl.pallas_call(
            functools.partial(kernel, nz, text),
            out_shape=(
                jax.ShapeDtypeStruct((tok, width), BF16),
                jax.ShapeDtypeStruct((att, tok), BF16),
                jax.ShapeDtypeStruct((att, tok), BF16),
            ),
            in_specs=[smem] + [vmem] * 4 + [hbm] * 8,
            out_specs=(hbm, hbm, hbm),
            scratch_shapes=scratch,
            compiler_params=pltpu.CompilerParams(
                collective_id=0, has_side_effects=True, vmem_limit_bytes=56 * 1024 * 1024
            ),
            cost_estimate=pl.CostEstimate(
                flops=2 * 10**9, bytes_accessed=6 * 10**6, transcendentals=6 * 10**6
            ),
        )(
            timestep,
            text_ids.reshape(1, text),
            text_table,
            norm_gain,
            norm_bias,
            latents,
            stale_keys.T,
            stale_values.T,
            time_weight,
            w_query.T,
            w_key.T,
            w_value.T,
            w_out,
        )
        return mixed, fresh_keys.T, fresh_values.T

    rows = P(("img", "patch"), None)
    return jax.shard_map(
        on_device,
        mesh=mesh,
        in_specs=(rows, rows, rows, P(), P("img"), P("patch", None)) + (P(),) * 7,
        out_specs=(rows, rows, rows),
        check_vma=False,
    )
```

time: 385 us -> 70.5 us (0.18)
  blocking collectives: 328 us -> 0 us
  Pallas kernels: 0 us -> 64.3 us
  matrix products: 23.7 us -> 0 us
  between operations: 14.9 us -> 1.29 us
  other arithmetic: 8.56 us -> 0 us
    psum x3 -> x0, blocking collectives: 328 us -> none  [the longest x1 115 us: on_device(): pooled = lax.psum(partial_pool, 'patch') / text_ids.shape[0]]
    pallas_call x0 -> x1, Pallas kernels: none -> 64.3 us  [on_device(): pl.pallas_call(functools.partial(kernel, nz, text), out_shape=(jax.ShapeD...]
    dot_general x10 -> x0, matrix products: 23.7 us -> none  [the longest x2 11.1 us: head_values(): return jnp.einsum('hqk,khd->hqd', probs, value_f)]
    reduce_sum x6 -> x0, other arithmetic: 7.79 us -> none  [the longest x1 5.54 us: on_device(): new_mass = mass * factor + jnp.sum(weights, axis=-1)]
  transfers between devices with their start and end apart: 2 -> 0, of which waited for: 0 -> 0; matrix products, arithmetic and copies ran while one was open for 5% -> 0% of each run, Pallas kernels for 0% -> 0%
where the time goes in v1:
time: 70.5 us; the launch traced here: 70.2 us
  Pallas kernels  64.3 us (91%)
  local copies, waits for them, and re-layouts  4.65 us (7%)
  between operations  1.29 us (2%)
    pallas_call x1, Pallas kernels, on_device(): pl.pallas_call(functools.partial(kernel, nz, text), out_shape=(jax.ShapeD...  64.3 us
    unnamed x3, local copies, waits for them, and re-layouts  4.65 us

profile of v1, /device:TPU:1, one launch (start us, length us, event | category | flops | bytes accessed | tf_op | source)
XLA Modules:
  0.0 70.2 jit_solution(4969528868901556403)
XLA Ops:
  1.3 64.3 %shard_map.148 = (bf16[128,640]{1,0:T(8,128)(2,1)}, bf16[320,128]{1,0:T(8,128)(2,1)}, bf16[320,128]{1,0:T(8,128)(2,1)}) custom-call(s32[1]{0:T(128)S(6)} %copy.19.time_ref, s32[1,77]{1,0:T(1,128)} %bitcast.15, bf16[386,1280]{1,0:T(8,128)(2,1)} %table_ref.1, f32[640]{0:T(1024)} %gain_ref.1, f32[640]{0:T(1024)} %bias_ref.1, bf16[128,640]{1,0:T(8,128)(2,1)} %lat_hbm.1, ...), custom_call_target="tpu_custom_call" | custom-call | flops 2000000000 | bytes 6000000 | tf_op jit(solution)/shard_map/pallas_call | solution.py:511
  65.6 1.6 %copy.20 = bf16[128,640]{1,0:T(8,128)(2,1)} copy(bf16[128,640]{1,0:T(8,128)(2,1)} %get-tuple-element.12) | data formatting | bytes 327680
  67.2 1.5 %copy.21 = bf16[128,320]{0,1:T(8,128)(2,1)} copy(bf16[128,320]{0,1:T(8,128)(2,1)} %bitcast.9) | data formatting | bytes 163840
  68.7 1.5 %copy.22 = bf16[128,320]{0,1:T(8,128)(2,1)} copy(bf16[128,320]{0,1:T(8,128)(2,1)} %bitcast.8) | data formatting | bytes 163840
